TPU v7x, 512 devices: a whole 4x8x8 slice. The times are simulated.
512 devices in a mesh: list: 16 (over z, core), sub: 8 (over y), slab: 4 (over x).
Axes of the slice: x: 4, y: 8, z: 8, core: 2. Of those that a mesh axis runs over, the one named last changes fastest.
Arguments:
- vectors: float32 [1024, 65536], P(None, ('list', 'sub', 'slab')), may hold values from -10 to 10
- centroids: bfloat16 [1024, 262144], P('sub', ('list', 'slab')), may hold values from -3 to 3
- codebook: float32 [32, 256, 32], P('sub'), may hold values from -10 to 10
- list_ids: int32 [65536], P(('list', 'sub', 'slab')), may hold values from 0 to 262143, as said below
Outputs:
- fresh_codebook: float32 [32, 256, 32], P('sub')
Inputs may be any that keep to these rules, and one draw needn't show every extreme that they name: `list_ids`: among the columns of one device, at most 4 name lists of one owner (list id // 4096); in every draw one owner receives exactly 4 from every device.
All inputs are finite; a program needn't handle non-finite values.
Results may differ from a plain program's by a relative error of at most 0.0003.
Values sent between devices are 32-bit elements; how exact they have to be, the bound alone decides.
A program may use at most 64 MiB of HBM per device.

v0:
```python
import math
import jax
import jax.numpy as jnp
from jax import lax
from jax.sharding import PartitionSpec as P

SOFTMAX_HEAT = 8.0
PRIOR_MASS = 1.0


def owner_rank(owner_of, owners):
    row_count = owner_of.shape[0]
    matches = (owner_of[:, None] == jnp.arange(owners)[None, :]).astype(jnp.float32)
    block = math.gcd(row_count, 128)
    blocks = matches.reshape(row_count // block, block, owners)
    strict_lower = (jnp.arange(block)[:, None] > jnp.arange(block)[None, :]).astype(jnp.float32)
    inside = jnp.einsum("ij,bjo->bio", strict_lower, blocks)
    totals = jnp.sum(blocks, axis=1)
    before = jnp.cumsum(totals, axis=0) - totals
    ranking = (inside + before[:, None, :]).reshape(row_count, owners)
    return jnp.sum(ranking * matches, axis=1).astype(jnp.int32)


def soft_sums(residual, weight, codebook):
    groups, num_codes, width = codebook.shape
    total_columns = residual.shape[1]
    block = math.gcd(total_columns, 1024)
    codeword_norm = jnp.sum(codebook * codebook, axis=-1)

    def block_step(loop_index, running):
        counts, weighted = running
        offset = (loop_index * block).astype(jnp.int32)
        column_piece = lax.dynamic_slice_in_dim(residual, offset, block, 1).reshape(
            groups, width, block
        )
        present = lax.dynamic_slice_in_dim(weight, offset, block, 0)
        inner_products = jnp.einsum(
            "skd,sdn->skn", codebook, column_piece, precision=lax.Precision.HIGHEST
        )
        assignment_scores = (2.0 * inner_products - codeword_norm[:, :, None]) / SOFTMAX_HEAT
        assignment_scores = assignment_scores - jnp.max(assignment_scores, axis=1, keepdims=True)
        exponent = jnp.exp(assignment_scores)
        assign = exponent / jnp.sum(exponent, axis=1, keepdims=True) * present[None, None, :]
        counts = counts + jnp.sum(assign, axis=2)
        weighted = weighted + jnp.einsum(
            "skn,sdn->skd", assign, column_piece, precision=lax.Precision.HIGHEST
        )
        return (counts, weighted)

    start_state = (
        jnp.zeros((groups, num_codes), jnp.float32),
        jnp.zeros((groups, num_codes, width), jnp.float32),
    )
    return lax.fori_loop(0, total_columns // block, block_step, start_state)


def refresh(counts, weighted, previous):
    return (weighted + PRIOR_MASS * previous) / (counts[:, :, None] + PRIOR_MASS)


def per_device(vectors, centroids, codebook, list_ids):
    list_count = lax.axis_size("list")
    slab_count = lax.axis_size("slab")
    sub_count = lax.axis_size("sub")
    owners = list_count * slab_count
    lists_here = centroids.shape[1]
    row_count = vectors.shape[1]
    capacity = 2 * row_count // owners
    owner_of = list_ids // lists_here
    within = (list_ids % lists_here).astype(jnp.float32)
    slot = owner_of * capacity + owner_rank(owner_of, owners)
    packed = jnp.zeros((vectors.shape[0], owners * capacity), jnp.float32).at[:, slot].set(vectors)
    labels = jnp.full((owners * capacity,), -1.0, jnp.float32).at[slot].set(within)
    labels = jnp.broadcast_to(labels[None, :], (sub_count, owners * capacity))
    arrived, arrived_labels = (
        lax.all_to_all(packed, ("list", "slab"), split_axis=1, concat_axis=1, tiled=True),
        lax.all_to_all(labels, ("list", "slab"), split_axis=1, concat_axis=1, tiled=True),
    )
    columns, column_labels = (
        lax.all_to_all(arrived, "sub", split_axis=0, concat_axis=1, tiled=True),
        lax.all_to_all(arrived_labels, "sub", split_axis=0, concat_axis=1, tiled=True),
    )
    final_labels = column_labels[0]
    present = final_labels >= 0.0
    weight = present.astype(jnp.float32)
    list_index = jnp.where(present, final_labels, 0.0).astype(jnp.int32)
    nearest = jnp.take(centroids, list_index, axis=1).astype(jnp.float32)
    residual = (columns - nearest) * weight[None, :]
    counts, weighted = soft_sums(residual, weight, codebook)
    counts, weighted = lax.psum((counts, weighted), ("list", "slab"))
    return refresh(counts, weighted, codebook)


def solution(mesh):
    return jax.shard_map(
        per_device,
        mesh=mesh,
        in_specs=(
            P(None, ("list", "sub", "slab")),
            P("sub", ("list", "slab")),
            P("sub", None, None),
            P(("list", "sub", "slab")),
        ),
        out_specs=P("sub", None, None),
        check_vma=False,
    )
```

profile of v0, /device:TPU:1, one launch (start us, length us, event | category | flops | bytes accessed | tf_op | source)
XLA Modules:
  0.0 453.4 jit_solution(12421118974912579844)
XLA Ops:
  7.5 1.0 scatter_custom_fusion.1
  9.4 14.8 %all-to-all-start.2 = ((f32[8,64,4]{0,2,1:T(4,128)}), f32[8,64,4]{0,2,1:T(4,128)S(1)}, u32[]{:S(2)}, u32[]{:S(2)}) async-start(f32[8,64,4]{0,2,1:T(4,128)} %broadcast_in_dim.61), calls=%async_computation.2 | async-start | bytes 262144 | tf_op jit(solution)/shard_map/all_to_all | solution.py:77
  24.2 1.2 copy.24
  25.5 1.3 scatter_custom_fusion
  26.8 1.3 all_to_all.34
  28.1 6.1 %all-to-all-done.2 = f32[8,64,4]{0,2,1:T(4,128)S(1)} async-done(((f32[8,64,4]{0,2,1:T(4,128)}), f32[8,64,4]{0,2,1:T(4,128)S(1)}, u32[]{:S(2)}, u32[]{:S(2)}) %all-to-all-start.2) | async-done | bytes 8224 | tf_op jit(solution)/shard_map/all_to_all | solution.py:77
  34.2 6.0 %all-to-all-start = ((f32[1024,64,4]{0,2,1:T(4,128)}), f32[1024,64,4]{0,2,1:T(4,128)S(1)}, u32[]{:S(2)}, u32[]{:S(2)}) async-start(f32[1024,64,4]{0,2,1:T(4,128)} %all_to_all.34), calls=%async_computation | async-start | bytes 2097152 | tf_op jit(solution)/shard_map/all_to_all | solution.py:76
  40.8 27.1 %all-to-all-done = f32[1024,64,4]{0,2,1:T(4,128)S(1)} async-done(((f32[1024,64,4]{0,2,1:T(4,128)}), f32[1024,64,4]{0,2,1:T(4,128)S(1)}, u32[]{:S(2)}, u32[]{:S(2)}) %all-to-all-start) | async-done | bytes 1048608 | tf_op jit(solution)/shard_map/all_to_all | solution.py:76
  68.0 6.8 %all-to-all-start.3 = ((f32[8,1,256]{2,1,0:T(1,128)}), f32[8,1,256]{2,1,0:T(1,128)S(1)}, u32[]{:S(2)}, u32[]{:S(2)}) async-start(f32[8,1,256]{2,1,0:T(1,128)} %copy.26), calls=%async_computation.3 | async-start | bytes 16384 | tf_op jit(solution)/shard_map/all_to_all | solution.py:81
  75.2 1.2 copy.25
  76.4 5.0 %all-to-all-done.3 = f32[8,1,256]{2,1,0:T(1,128)S(1)} async-done(((f32[8,1,256]{2,1,0:T(1,128)}), f32[8,1,256]{2,1,0:T(1,128)S(1)}, u32[]{:S(2)}, u32[]{:S(2)}) %all-to-all-start.3) | async-done | bytes 8224 | tf_op jit(solution)/shard_map/all_to_all | solution.py:81
  81.4 3.6 all-to-all-start.1
  85.9 6.2 %gather_fusion = bf16[2048,128]{1,0:T(8,128)(2,1)S(1)} fusion(bf16[128,4096]{0,1:T(8,128)(2,1)S(1)} %copy.27, s32[2048]{0:T(1024)S(1)} %broadcast_clamp_fusion), kind=kCustom, calls=%fused_computation | custom fusion | bytes 1056768 | tf_op jit(solution)/shard_map/jit(_take)/gather | solution.py:87
  92.1 19.6 %all-to-all-done.1 = f32[8,128,256]{1,2,0:T(8,128)S(1)} async-done(((f32[8,128,256]{1,2,0:T(8,128)}), f32[8,128,256]{1,2,0:T(8,128)S(1)}, u32[]{:S(2)}, u32[]{:S(2)}) %all-to-all-start.1) | async-done | bytes 1048608 | tf_op jit(solution)/shard_map/all_to_all | solution.py:80
  112.5 27.6 %while.16 = (s32[]{:T(128)}, f32[4,256]{1,0:T(4,128)S(1)}, f32[4,256,32]{1,2,0:T(8,128)S(1)}, f32[128,2048]{0,1:T(8,128)S(1)}, f32[4,256,32]{1,2,0:T(8,128)S(1)}...) while((s32[]{:T(128)}, f32[4,256]{1,0:T(4,128)S(1)}, ...), condition=%wide.region_9.10_spmd.clone, body=%wide.region_5.9_spmd.clone.sunk | while | flops 819004672 | bytes 41373896 | solution.py:54
  112.8 3.5 fusion.41
  116.2 3.0 fusion.42
  119.2 6.5 %fusion.44 = f32[4,256,32]{1,2,0:T(8,128)S(1)} fusion(f32[4,32,1024]{2,1,0:T(8,128)S(1)} %bitcast.61, f32[4,256,1024]{2,1,0:T(8,128)} %get-tuple-element.256, f32[1024]{0:T(1024)S(1)} %dynamic_slice.20, f32[4,1024]{1,0:T(4,128)S(1)} %get-tuple-element.257, f32[4,256,32]{1,2,0:T(8,128)S(1)} %get-tuple-element.271, pred[]{:T(512)S(6)} %compare.6), kind=kOutput, calls=%fused_computation.15.clone.1 | convolution fusion | flops 404815872 | bytes 5001217 | tf_op jit(solution)/shard_map/while/body/eval_jaxpr/skn,sdn->skd/dot_general | solution.py:45
  126.6 3.5 fusion.41
  130.0 3.0 fusion.42
  133.0 6.5 %fusion.44 = f32[4,256,32]{1,2,0:T(8,128)S(1)} fusion(f32[4,32,1024]{2,1,0:T(8,128)S(1)} %bitcast.61, f32[4,256,1024]{2,1,0:T(8,128)} %get-tuple-element.256, f32[1024]{0:T(1024)S(1)} %dynamic_slice.20, f32[4,1024]{1,0:T(4,128)S(1)} %get-tuple-element.257, f32[4,256,32]{1,2,0:T(8,128)S(1)} %get-tuple-element.271, pred[]{:T(512)S(6)} %compare.6), kind=kOutput, calls=%fused_computation.15.clone.1 | convolution fusion | flops 404815872 | bytes 5001217 | tf_op jit(solution)/shard_map/while/body/eval_jaxpr/skn,sdn->skd/dot_general | solution.py:45
  140.1 123.2 %psum.15 = f32[4,256]{1,0:T(4,128)S(1)} all-reduce(f32[4,256]{1,0:T(4,128)S(1)} %get-tuple-element.131), channel_id=1, replica_groups=mesh['list'=16,'sub'=8,'slab'=4] {'list','slab'}, use_global_device_ids=true, to_apply=%region_11.12 | all-reduce | flops 1024 | bytes 8192 | tf_op jit(solution)/shard_map/psum | solution.py:90
  263.4 181.7 %all-reduce.2.cloned.1.call-done = f32[4,256,32]{1,2,0:T(8,128)} async-done(((f32[4,256,32]{1,2,0:T(8,128)}), f32[4,256,32]{1,2,0:T(8,128)}) %all-reduce.2.cloned.1.call-update) | async-done | bytes 131088 | tf_op jit(solution)/shard_map/psum | solution.py:90
  445.0 1.6 add_divide_fusion
  (40 shorter events, 6.2 us)
Async XLA Ops:
  9.4 24.8 %all-to-all-start.2 = ((f32[8,64,4]{0,2,1:T(4,128)}), f32[8,64,4]{0,2,1:T(4,128)S(1)}, u32[]{:S(2)}, u32[]{:S(2)}) async-start(f32[8,64,4]{0,2,1:T(4,128)} %broadcast_in_dim.61), calls=%async_computation.2 | async-start | bytes 262144 | tf_op jit(solution)/shard_map/all_to_all | solution.py:77
  28.1 57.1 %copy-start.2 = (bf16[128,4096]{1,0:T(8,128)(2,1)S(1)}, bf16[128,4096]{1,0:T(8,128)(2,1)}, u32[]{:S(2)}) copy-start(bf16[128,4096]{1,0:T(8,128)(2,1)} %param.7) | copy-start | bytes 3145732
  34.2 33.8 %all-to-all-start = ((f32[1024,64,4]{0,2,1:T(4,128)}), f32[1024,64,4]{0,2,1:T(4,128)S(1)}, u32[]{:S(2)}, u32[]{:S(2)}) async-start(f32[1024,64,4]{0,2,1:T(4,128)} %all_to_all.34), calls=%async_computation | async-start | bytes 2097152 | tf_op jit(solution)/shard_map/all_to_all | solution.py:76
  68.0 13.4 %all-to-all-start.3 = ((f32[8,1,256]{2,1,0:T(1,128)}), f32[8,1,256]{2,1,0:T(1,128)S(1)}, u32[]{:S(2)}, u32[]{:S(2)}) async-start(f32[8,1,256]{2,1,0:T(1,128)} %copy.26), calls=%async_computation.3 | async-start | bytes 16384 | tf_op jit(solution)/shard_map/all_to_all | solution.py:81
  74.8 11.1 %copy-start.1 = (f32[4,256,32]{1,2,0:T(8,128)S(1)}, f32[4,256,32]{1,2,0:T(8,128)}, u32[]{:S(2)}) copy-start(f32[4,256,32]{1,2,0:T(8,128)} %param.8) | copy-start | bytes 393220
  81.4 30.4 %all-to-all-start.1 = ((f32[8,128,256]{1,2,0:T(8,128)}), f32[8,128,256]{1,2,0:T(8,128)S(1)}, u32[]{:S(2)}, u32[]{:S(2)}) async-start(f32[8,128,256]{1,2,0:T(8,128)} %copy.25), calls=%async_computation.1 | async-start | bytes 2097152 | tf_op jit(solution)/shard_map/all_to_all | solution.py:80
  84.9 360.1 %all-reduce.2.cloned.1.call-start = ((), (), s32[]{:S(2)}) async-start(), calls=%async_computation.4 | async-start | bytes 262144 | tf_op jit(solution)/shard_map/psum | solution.py:90
  119.2 6.5 %copy-start = (f32[4,256,1024]{2,1,0:T(8,128)S(1)}, f32[4,256,1024]{2,1,0:T(8,128)}, u32[]{:S(2)}) copy-start(f32[4,256,1024]{2,1,0:T(8,128)} %get-tuple-element.256) | copy-start | bytes 12582916 | tf_op jit(solution)/shard_map/while
  133.0 6.5 %copy-start = (f32[4,256,1024]{2,1,0:T(8,128)S(1)}, f32[4,256,1024]{2,1,0:T(8,128)}, u32[]{:S(2)}) copy-start(f32[4,256,1024]{2,1,0:T(8,128)} %get-tuple-element.256) | copy-start | bytes 12582916 | tf_op jit(solution)/shard_map/while
  140.1 123.2 %copy-start.3 = (f32[4,256,32]{1,2,0:T(8,128)}, f32[4,256,32]{1,2,0:T(8,128)S(1)}, u32[]{:S(2)}) copy-start(f32[4,256,32]{1,2,0:T(8,128)S(1)} %get-tuple-element.130) | copy-start | bytes 393220
Sparse Core Ops, SparseCore 0:
  263.5 181.4 all-reduce.1
where the time goes:
time: 454 us; the launch traced here: 453 us
  waiting for transfers between devices  239 us (53%)
  blocking collectives  123 us (27%)
  starting transfers between devices  31.4 us (7%)
  matrix products  20.1 us (4%)
  local copies, waits for them, and re-layouts  15.3 us (3%)
  between operations  13.6 us (3%)
  other arithmetic  10.2 us (2%)
    psum x1, waiting for transfers between devices, per_device(): counts, weighted = lax.psum((counts, weighted), ('list', 'slab'))  182 us
    psum x1, blocking collectives, per_device(): counts, weighted = lax.psum((counts, weighted), ('list', 'slab'))  123 us
    all_to_all x1, waiting for transfers between devices, per_device(): lax.all_to_all(packed, ('list', 'slab'), split_axis=1, concat_axis=1, til...  27.1 us
    all_to_all x1, waiting for transfers between devices, per_device(): lax.all_to_all(arrived, 'sub', split_axis=0, concat_axis=1, tiled=True)  19.6 us
    all_to_all x1, starting transfers between devices, per_device(): lax.all_to_all(labels, ('list', 'slab'), split_axis=1, concat_axis=1, til...  14.8 us
    dot_general x2, matrix products, block_step(): jnp.einsum('skn,sdn->skd', assign, column_piece, precision=lax.Precision....  13 us
  transfers between devices with their start and end apart: 5, of which 5 were waited for; matrix products, arithmetic and copies ran while one was open for 2% of the time, Pallas kernels for 0%

commit v1 on v0

--- a/solution.py
+++ b/solution.py
@@ -6,6 +6,11 @@
 
 SOFTMAX_HEAT = 8.0
 PRIOR_MASS = 1.0
+
+
+def axis_by_axis(value, axis_one, axis_two):
+    inner = lax.psum(value, axis_one)
+    return lax.psum(inner, axis_two)
 
 
 def owner_rank(owner_of, owners):
@@ -87,7 +92,7 @@
     nearest = jnp.take(centroids, list_index, axis=1).astype(jnp.float32)
     residual = (columns - nearest) * weight[None, :]
     counts, weighted = soft_sums(residual, weight, codebook)
-    counts, weighted = lax.psum((counts, weighted), ("list", "slab"))
+    counts, weighted = axis_by_axis((counts, weighted), "list", "slab")
     return refresh(counts, weighted, codebook)
 
 

time: 454 us -> 311 us (0.69)
  blocking collectives: 123 us -> 34 us
  waiting for transfers between devices: 239 us -> 184 us
    psum x1 -> x2, blocking collectives: 123 us -> 34 us  [the longest x1 25.8 us: axis_by_axis(): inner = lax.psum(value, axis_one)]
    psum x1 -> x2, waiting for transfers between devices: 182 us -> 126 us  [the longest x1 74.4 us: axis_by_axis(): inner = lax.psum(value, axis_one)]
  transfers between devices with their start and end apart: 5 -> 6, of which waited for: 5 -> 6; matrix products, arithmetic and copies ran while one was open for 2% -> 4% of each run, Pallas kernels for 0% -> 0%
where the time goes in v1:
time: 311 us; the launch traced here: 310 us
  waiting for transfers between devices  184 us (59%)
  blocking collectives  34 us (11%)
  starting transfers between devices  31.5 us (10%)
  matrix products  20.1 us (6%)
  local copies, waits for them, and re-layouts  15.9 us (5%)
  between operations  13.6 us (4%)
  other arithmetic  10.2 us (3%)
    psum x1, waiting for transfers between devices, axis_by_axis(): inner = lax.psum(value, axis_one)  74.4 us
    psum x1, waiting for transfers between devices, axis_by_axis(): return lax.psum(inner, axis_two)  51.9 us
    all_to_all x1, waiting for transfers between devices, per_device(): lax.all_to_all(packed, ('list', 'slab'), split_axis=1, concat_axis=1, til...  27.1 us
    psum x1, blocking collectives, axis_by_axis(): inner = lax.psum(value, axis_one)  25.8 us
    all_to_all x1, waiting for transfers between devices, per_device(): lax.all_to_all(arrived, 'sub', split_axis=0, concat_axis=1, tiled=True)  19.6 us
    all_to_all x1, starting transfers between devices, per_device(): lax.all_to_all(labels, ('list', 'slab'), split_axis=1, concat_axis=1, til...  14.8 us
    dot_general x2, matrix products, block_step(): jnp.einsum('skn,sdn->skd', assign, column_piece, precision=lax.Precision....  13 us
    psum x1, blocking collectives, axis_by_axis(): return lax.psum(inner, axis_two)  8.28 us
  transfers between devices with their start and end apart: 6, of which 6 were waited for; matrix products, arithmetic and copies ran while one was open for 4% of the time, Pallas kernels for 0%

profile of v1, /device:TPU:1, one launch (start us, length us, event | category | flops | bytes accessed | tf_op | source)
XLA Modules:
  0.0 309.6 jit_solution(15459681026933057030)
XLA Ops:
  9.4 14.8 %all-to-all-start.2 = ((f32[8,64,4]{0,2,1:T(4,128)}), f32[8,64,4]{0,2,1:T(4,128)S(1)}, u32[]{:S(2)}, u32[]{:S(2)}) async-start(f32[8,64,4]{0,2,1:T(4,128)} %broadcast_in_dim.61), calls=%async_computation.2 | async-start | bytes 262144 | tf_op jit(solution)/shard_map/all_to_all | solution.py:82
  24.2 1.2 copy.24
  25.5 1.3 scatter_custom_fusion
  26.8 1.3 all_to_all.34
  28.1 6.1 %all-to-all-done.2 = f32[8,64,4]{0,2,1:T(4,128)S(1)} async-done(((f32[8,64,4]{0,2,1:T(4,128)}), f32[8,64,4]{0,2,1:T(4,128)S(1)}, u32[]{:S(2)}, u32[]{:S(2)}) %all-to-all-start.2) | async-done | bytes 8224 | tf_op jit(solution)/shard_map/all_to_all | solution.py:82
  34.2 6.0 %all-to-all-start = ((f32[1024,64,4]{0,2,1:T(4,128)}), f32[1024,64,4]{0,2,1:T(4,128)S(1)}, u32[]{:S(2)}, u32[]{:S(2)}) async-start(f32[1024,64,4]{0,2,1:T(4,128)} %all_to_all.34), calls=%async_computation | async-start | bytes 2097152 | tf_op jit(solution)/shard_map/all_to_all | solution.py:81
  40.8 27.1 %all-to-all-done = f32[1024,64,4]{0,2,1:T(4,128)S(1)} async-done(((f32[1024,64,4]{0,2,1:T(4,128)}), f32[1024,64,4]{0,2,1:T(4,128)S(1)}, u32[]{:S(2)}, u32[]{:S(2)}) %all-to-all-start) | async-done | bytes 1048608 | tf_op jit(solution)/shard_map/all_to_all | solution.py:81
  68.0 6.8 %all-to-all-start.3 = ((f32[8,1,256]{2,1,0:T(1,128)}), f32[8,1,256]{2,1,0:T(1,128)S(1)}, u32[]{:S(2)}, u32[]{:S(2)}) async-start(f32[8,1,256]{2,1,0:T(1,128)} %copy.26), calls=%async_computation.3 | async-start | bytes 16384 | tf_op jit(solution)/shard_map/all_to_all | solution.py:86
  76.4 5.0 %all-to-all-done.3 = f32[8,1,256]{2,1,0:T(1,128)S(1)} async-done(((f32[8,1,256]{2,1,0:T(1,128)}), f32[8,1,256]{2,1,0:T(1,128)S(1)}, u32[]{:S(2)}, u32[]{:S(2)}) %all-to-all-start.3) | async-done | bytes 8224 | tf_op jit(solution)/shard_map/all_to_all | solution.py:86
  81.4 3.6 %all-to-all-start.1 = ((f32[8,128,256]{1,2,0:T(8,128)}), f32[8,128,256]{1,2,0:T(8,128)S(1)}, u32[]{:S(2)}, u32[]{:S(2)}) async-start(f32[8,128,256]{1,2,0:T(8,128)} %copy.25), calls=%async_computation.1 | async-start | bytes 2097152 | tf_op jit(solution)/shard_map/all_to_all | solution.py:85
  85.9 6.2 %gather_fusion = bf16[2048,128]{1,0:T(8,128)(2,1)S(1)} fusion(bf16[128,4096]{0,1:T(8,128)(2,1)S(1)} %copy.27, s32[2048]{0:T(1024)S(1)} %broadcast_clamp_fusion), kind=kCustom, calls=%fused_computation | custom fusion | bytes 1056768 | tf_op jit(solution)/shard_map/jit(_take)/gather | solution.py:92
  92.1 19.6 %all-to-all-done.1 = f32[8,128,256]{1,2,0:T(8,128)S(1)} async-done(((f32[8,128,256]{1,2,0:T(8,128)}), f32[8,128,256]{1,2,0:T(8,128)S(1)}, u32[]{:S(2)}, u32[]{:S(2)}) %all-to-all-start.1) | async-done | bytes 1048608 | tf_op jit(solution)/shard_map/all_to_all | solution.py:85
  112.5 27.6 %while.16 = (s32[]{:T(128)}, f32[4,256]{1,0:T(4,128)S(1)}, f32[4,256,32]{1,2,0:T(8,128)S(1)}, f32[128,2048]{0,1:T(8,128)S(1)}, f32[4,256,32]{1,2,0:T(8,128)S(1)}...) while((s32[]{:T(128)}, f32[4,256]{1,0:T(4,128)S(1)}, ...), condition=%wide.region_9.10_spmd.clone, body=%wide.region_5.9_spmd.clone.sunk | while | flops 819004672 | bytes 41373896 | solution.py:59
  112.8 3.5 %fusion.41 = f32[4,1024,256]{1,2,0:T(8,128)S(1)} fusion(f32[4,32,1024]{2,1,0:T(8,128)S(1)} %bitcast.60, f32[4,256,32]{1,2,0:T(8,128)S(1)} %get-tuple-element.284), kind=kOutput, calls=%fused_computation.56.clone.1 | convolution fusion | flops 402653184 | bytes 4849664 | tf_op jit(solution)/shard_map/while/body/eval_jaxpr/skd,sdn->skn/dot_general | solution.py:42
  116.2 3.0 fusion.42
  119.2 6.5 %fusion.44 = f32[4,256,32]{1,2,0:T(8,128)S(1)} fusion(f32[4,32,1024]{2,1,0:T(8,128)S(1)} %bitcast.61, f32[4,256,1024]{2,1,0:T(8,128)} %get-tuple-element.256, f32[1024]{0:T(1024)S(1)} %dynamic_slice.20, f32[4,1024]{1,0:T(4,128)S(1)} %get-tuple-element.257, f32[4,256,32]{1,2,0:T(8,128)S(1)} %get-tuple-element.271, pred[]{:T(512)S(6)} %compare.6), kind=kOutput, calls=%fused_computation.15.clone.1 | convolution fusion | flops 404815872 | bytes 5001217 | tf_op jit(solution)/shard_map/while/body/eval_jaxpr/skn,sdn->skd/dot_general | solution.py:50
  126.6 3.5 %fusion.41 = f32[4,1024,256]{1,2,0:T(8,128)S(1)} fusion(f32[4,32,1024]{2,1,0:T(8,128)S(1)} %bitcast.60, f32[4,256,32]{1,2,0:T(8,128)S(1)} %get-tuple-element.284), kind=kOutput, calls=%fused_computation.56.clone.1 | convolution fusion | flops 402653184 | bytes 4849664 | tf_op jit(solution)/shard_map/while/body/eval_jaxpr/skd,sdn->skn/dot_general | solution.py:42
  130.0 3.0 fusion.42
  133.0 6.5 %fusion.44 = f32[4,256,32]{1,2,0:T(8,128)S(1)} fusion(f32[4,32,1024]{2,1,0:T(8,128)S(1)} %bitcast.61, f32[4,256,1024]{2,1,0:T(8,128)} %get-tuple-element.256, f32[1024]{0:T(1024)S(1)} %dynamic_slice.20, f32[4,1024]{1,0:T(4,128)S(1)} %get-tuple-element.257, f32[4,256,32]{1,2,0:T(8,128)S(1)} %get-tuple-element.271, pred[]{:T(512)S(6)} %compare.6), kind=kOutput, calls=%fused_computation.15.clone.1 | convolution fusion | flops 404815872 | bytes 5001217 | tf_op jit(solution)/shard_map/while/body/eval_jaxpr/skn,sdn->skd/dot_general | solution.py:50
  140.8 25.8 %psum.30 = f32[4,256]{1,0:T(4,128)S(1)} all-reduce(f32[4,256]{1,0:T(4,128)S(1)} %get-tuple-element.131), channel_id=1, replica_groups=mesh['list'=16,'sub'=8,'slab'=4] {'list'}, use_global_device_ids=true, to_apply=%region_12.13 | all-reduce | flops 1024 | bytes 8192 | tf_op jit(solution)/shard_map/psum | solution.py:12
  166.6 8.3 %psum.31 = f32[4,256]{1,0:T(4,128)S(1)} all-reduce(f32[4,256]{1,0:T(4,128)S(1)} %psum.30), channel_id=1, replica_groups=mesh['list'=16,'sub'=8,'slab'=4] {'slab'}, use_global_device_ids=true, to_apply=%region_13.14 | all-reduce | flops 1024 | bytes 8192 | tf_op jit(solution)/shard_map/psum | solution.py:13
  174.9 74.4 %all-reduce.3.cloned.1.call-done = f32[4,256,32]{1,2,0:T(8,128)} async-done(((f32[4,256,32]{1,2,0:T(8,128)}), f32[4,256,32]{1,2,0:T(8,128)}) %all-reduce.3.cloned.1.call-update) | async-done | bytes 131088 | tf_op jit(solution)/shard_map/psum | solution.py:12
  249.3 51.9 %all-reduce.5.cloned.1.call-done = f32[4,256,32]{1,2,0:T(8,128)} async-done(((f32[4,256,32]{1,2,0:T(8,128)}), f32[4,256,32]{1,2,0:T(8,128)}) %all-reduce.5.cloned.1.call-update) | async-done | bytes 131088 | tf_op jit(solution)/shard_map/psum | solution.py:13
  301.2 1.6 add_divide_fusion
  (44 shorter events, 9.1 us)
Async XLA Ops:
  9.4 24.8 %all-to-all-start.2 = ((f32[8,64,4]{0,2,1:T(4,128)}), f32[8,64,4]{0,2,1:T(4,128)S(1)}, u32[]{:S(2)}, u32[]{:S(2)}) async-start(f32[8,64,4]{0,2,1:T(4,128)} %broadcast_in_dim.61), calls=%async_computation.2 | async-start | bytes 262144 | tf_op jit(solution)/shard_map/all_to_all | solution.py:82
  28.1 57.1 %copy-start.2 = (bf16[128,4096]{1,0:T(8,128)(2,1)S(1)}, bf16[128,4096]{1,0:T(8,128)(2,1)}, u32[]{:S(2)}) copy-start(bf16[128,4096]{1,0:T(8,128)(2,1)} %param.7) | copy-start | bytes 3145732
  34.2 33.8 %all-to-all-start = ((f32[1024,64,4]{0,2,1:T(4,128)}), f32[1024,64,4]{0,2,1:T(4,128)S(1)}, u32[]{:S(2)}, u32[]{:S(2)}) async-start(f32[1024,64,4]{0,2,1:T(4,128)} %all_to_all.34), calls=%async_computation | async-start | bytes 2097152 | tf_op jit(solution)/shard_map/all_to_all | solution.py:81
  68.0 13.4 %all-to-all-start.3 = ((f32[8,1,256]{2,1,0:T(1,128)}), f32[8,1,256]{2,1,0:T(1,128)S(1)}, u32[]{:S(2)}, u32[]{:S(2)}) async-start(f32[8,1,256]{2,1,0:T(1,128)} %copy.26), calls=%async_computation.3 | async-start | bytes 16384 | tf_op jit(solution)/shard_map/all_to_all | solution.py:86
  74.8 11.1 %copy-start.1 = (f32[4,256,32]{1,2,0:T(8,128)S(1)}, f32[4,256,32]{1,2,0:T(8,128)}, u32[]{:S(2)}) copy-start(f32[4,256,32]{1,2,0:T(8,128)} %param.8) | copy-start | bytes 393220
  81.4 30.4 %all-to-all-start.1 = ((f32[8,128,256]{1,2,0:T(8,128)}), f32[8,128,256]{1,2,0:T(8,128)S(1)}, u32[]{:S(2)}, u32[]{:S(2)}) async-start(f32[8,128,256]{1,2,0:T(8,128)} %copy.25), calls=%async_computation.1 | async-start | bytes 2097152 | tf_op jit(solution)/shard_map/all_to_all | solution.py:85
  84.9 164.3 %all-reduce.3.cloned.1.call-start = ((), (), s32[]{:S(2)}) async-start(), calls=%async_computation.4 | async-start | bytes 262144 | tf_op jit(solution)/shard_map/psum | solution.py:12
  119.2 6.5 %copy-start = (f32[4,256,1024]{2,1,0:T(8,128)S(1)}, f32[4,256,1024]{2,1,0:T(8,128)}, u32[]{:S(2)}) copy-start(f32[4,256,1024]{2,1,0:T(8,128)} %get-tuple-element.256) | copy-start | bytes 12582916 | tf_op jit(solution)/shard_map/while
  133.0 6.5 %copy-start = (f32[4,256,1024]{2,1,0:T(8,128)S(1)}, f32[4,256,1024]{2,1,0:T(8,128)}, u32[]{:S(2)}) copy-start(f32[4,256,1024]{2,1,0:T(8,128)} %get-tuple-element.256) | copy-start | bytes 12582916 | tf_op jit(solution)/shard_map/while
  140.1 0.7 copy-start.3
  140.8 160.4 %all-reduce.5.cloned.1.call-start = ((), (), s32[]{:S(2)}) async-start(), calls=%async_computation.5 | async-start | bytes 262144 | tf_op jit(solution)/shard_map/psum | solution.py:13
Sparse Core Ops, SparseCore 0:
  140.9 108.2 all-reduce.2
  251.7 49.4 all-reduce.4
